TPU v7x, 512 devices: a whole 4x8x8 slice. The times are simulated.
512 devices in a mesh: pool: 16 (over z_lo, y), tp: 32 (over x, z_hi, core).
Axes of the slice: x: 4, y: 8, z: 8 (z_hi: 4, z_lo: 2; z = z_hi * 2 + z_lo), core: 2. Of those that a mesh axis runs over, the one named last changes fastest.
Arguments:
- page_store: bfloat16 [8192, 64, 576], P(('pool', 'tp')), may hold values from -6.5 to 6.5
- page_table: int32 [128, 64], replicated, may hold values from 0 to 8191, as said below
- context_len: int32 [128], replicated, may hold values from 1 to 4096, 393216 in all
- absorbed_query: bfloat16 [128, 64, 576], P('pool', 'tp'), may hold values from -8 to 8
- value_up: bfloat16 [64, 512, 128], P('tp'), may hold values from -0.25 to 0.25
- out_proj: bfloat16 [8192, 7168], P('tp', 'pool'), may hold values from -0.0625 to 0.0625
Outputs:
- attn_output: bfloat16 [128, 7168], P('tp', 'pool')
Inputs may be any that keep to these rules, and one draw needn't show every extreme that they name: `page_table`: every slot of page_store is named exactly once. The 16 slots held by one device of pool+tp name exactly 1 pages of requests of each decode group (requests g * 8 to (g + 1) * 8 - 1 form group g). Page j of request g * 8 + i has q = i * 64 + j and lies in a slot of a device whose tp index is q // 16.
All inputs are finite; a program needn't handle non-finite values.
Results may differ from a plain program's by a relative error of at most 0.015.
Values may be sent and summed in bfloat16 or wider, within the bound.
A program may use at most 128 MiB of HBM per device.

v0:
```python
import jax
import jax.numpy as jnp
from jax import lax
from jax.sharding import PartitionSpec as P

score_scale = 192.0 ** (-0.5)
masked_score = -1e30


def joined(array, axis, combine):
    everything = jax.tree.map(lambda part: lax.all_gather(part, axis), array)
    initial = jax.tree.map(lambda part: part[0], everything)

    def turn(k, so_far):
        return combine(so_far, jax.tree.map(lambda part: part[k], everything))

    return lax.fori_loop(1, lax.axis_size(axis), turn, initial)


def packing_order(slot_codes, group_pages, pool_count, per_group):
    destination = slot_codes // group_pages
    member = (destination[:, None] == jnp.arange(pool_count, dtype=jnp.int32)[None, :]).astype(
        jnp.int32
    )
    within_rank = jnp.sum(member * (jnp.cumsum(member, axis=0) - 1), axis=1)
    return jnp.argsort(destination * per_group + within_rank)


def combine_parts(left_part, right_part):
    joined_top = jnp.maximum(left_part[0], right_part[0])
    left_factor = jnp.exp(left_part[0] - joined_top)
    right_factor = jnp.exp(right_part[0] - joined_top)
    joined_total = left_part[1] * left_factor + right_part[1] * right_factor
    joined_mixed = left_part[2] * left_factor[..., None] + right_part[2] * right_factor[..., None]
    return (joined_top, joined_total, joined_mixed)


def dense_partials(query_rows, member, live_mask, arrived, latent_width):
    scores = jnp.einsum("rhk,pik->rhpi", query_rows, arrived, preferred_element_type=jnp.float32)
    usable = member[:, None, :, None] & live_mask[None, None, :, :]
    scores = jnp.where(usable, scores * score_scale, masked_score)
    page_top = jnp.max(scores, axis=-1)
    weights = jnp.where(usable, jnp.exp(scores - page_top[..., None]), 0.0)
    page_total = jnp.sum(weights, axis=-1)
    page_mixed = jnp.einsum(
        "rhpi,pil->rhpl",
        weights.astype(jnp.bfloat16),
        arrived[:, :, :latent_width],
        preferred_element_type=jnp.float32,
    )
    row_top = jnp.max(page_top, axis=-1)
    factor = jnp.exp(page_top - row_top[..., None])
    weight_total = jnp.sum(factor * page_total, axis=-1)
    mixed = jnp.einsum("rhp,rhpl->rhl", factor, page_mixed, precision=lax.Precision.HIGHEST)
    return (row_top, weight_total, mixed)


def per_device(page_store, page_table, context_len, absorbed_query, value_up, out_proj):
    pool_count = lax.axis_size("pool")
    tp_count = lax.axis_size("tp")
    pool_index = lax.axis_index("pool")
    tp_index = lax.axis_index("tp")
    pages_held, page_tokens, key_width = page_store.shape
    group_requests, local_heads, _ = absorbed_query.shape
    pages_request = page_table.shape[1]
    group_pages = group_requests * pages_request
    per_group = pages_held // pool_count
    latent_width = value_up.shape[1]
    flat_table = page_table.reshape(-1)
    slot_owner = (
        jnp.zeros((flat_table.shape[0],), jnp.int32)
        .at[flat_table]
        .set(jnp.arange(flat_table.shape[0], dtype=jnp.int32))
    )
    my_start = (pool_index * tp_count + tp_index) * pages_held
    my_codes = lax.dynamic_slice_in_dim(slot_owner, my_start, pages_held)
    send_order = packing_order(my_codes, group_pages, pool_count, per_group)
    outgoing = jnp.take(page_store, send_order, axis=0)
    arrived = lax.all_to_all(outgoing, "pool", split_axis=0, concat_axis=0, tiled=True)
    peer_starts = (jnp.arange(pool_count, dtype=jnp.int32) * tp_count + tp_index) * pages_held
    peer_codes = slot_owner[peer_starts[:, None] + jnp.arange(pages_held, dtype=jnp.int32)[None, :]]
    peer_orders = jax.vmap(
        lambda codes_row: packing_order(codes_row, group_pages, pool_count, per_group)
    )(peer_codes)
    sorted_codes = jnp.take_along_axis(peer_codes, peer_orders, axis=1)
    arrived_codes = lax.dynamic_slice_in_dim(
        sorted_codes, pool_index * per_group, per_group, 1
    ).reshape(-1)
    slot_request = arrived_codes // pages_request - pool_index * group_requests
    slot_page = arrived_codes % pages_request
    lengths = lax.dynamic_slice_in_dim(context_len, pool_index * group_requests, group_requests)
    positions = slot_page[:, None] * page_tokens + jnp.arange(page_tokens, dtype=jnp.int32)[None, :]
    live_mask = positions < jnp.take(lengths, slot_request)[:, None]
    all_queries = lax.all_gather(absorbed_query, "tp", axis=1, tiled=True)
    member = slot_request[None, :] == jnp.arange(group_requests, dtype=jnp.int32)[:, None]
    row_top, weight_total, mixed = dense_partials(
        all_queries, member, live_mask, arrived, latent_width
    )
    joined_top, joined_total, joined_mixed = joined(
        (row_top, weight_total, mixed), "tp", combine_parts
    )
    head_start = tp_index * local_heads
    own_total = lax.dynamic_slice_in_dim(joined_total, head_start, local_heads, 1)
    own_mixed = lax.dynamic_slice_in_dim(joined_mixed, head_start, local_heads, 1)
    attended = own_mixed / own_total[..., None]
    attended = attended.astype(jnp.bfloat16)
    head_output = jnp.einsum("rhl,hlv->rhv", attended, value_up, preferred_element_type=jnp.float32)
    head_output = head_output.astype(jnp.bfloat16).reshape(group_requests, -1)
    all_requests = lax.all_gather(head_output, "pool", axis=0, tiled=True)
    summed = lax.psum_scatter(
        jnp.dot(all_requests, out_proj, preferred_element_type=jnp.float32),
        "tp",
        scatter_dimension=0,
        tiled=True,
    )
    return summed.astype(jnp.bfloat16)


def solution(mesh):
    placed = (
        P(("pool", "tp"), None, None),
        P(),
        P(),
        P("pool", "tp", None),
        P("tp", None, None),
        P("tp", "pool"),
    )
    return jax.shard_map(
        per_device, mesh=mesh, in_specs=placed, out_specs=P("tp", "pool"), check_vma=False
    )
```

profile of v0, /device:TPU:1, one launch (start us, length us, event | category | flops | bytes accessed | tf_op | source)
XLA Modules:
  0.0 578.8 jit_solution(3203669846105277513)
XLA Ops:
  7.8 30.5 %scatter_custom_fusion = s32[8192]{0:T(1024)S(1)} fusion(s32[8192]{0:T(1024)S(1)} %bitcast.79, s32[8192]{0:T(1024)S(1)} %iota.43, s32[]{:T(128)} %constant.148.clone.1), kind=kCustom, calls=%fused_computation.46 | custom fusion | bytes 32772 | tf_op jit(solution)/shard_map/scatter | solution.py:73
  38.3 1.7 gather_fusion
  41.7 1.9 gather_fusion.3
  48.8 9.6 %all-to-all-start = ((bf16[16,64,576]{2,1,0:T(8,128)(2,1)}), bf16[16,64,576]{2,1,0:T(8,128)(2,1)S(1)}, u32[]{:S(2)}, u32[]{:S(2)}) async-start(bf16[16,64,576]{2,1,0:T(8,128)(2,1)} %broadcast_select_fusion), calls=%async_computation | async-start | bytes 2621440 | tf_op jit(solution)/shard_map/all_to_all | solution.py:79
  58.7 52.5 %all_gather.24 = bf16[8,64,576]{2,0,1:T(8,128)(2,1)S(1)} all-gather(bf16[8,2,576]{2,0,1:T(8,128)(2,1)S(1)} %copy.38), channel_id=1, replica_groups=mesh['pool'=16,'tp'=32] {'tp'}, dimensions={1}, use_global_device_ids=true | all-gather | bytes 608256 | tf_op jit(solution)/shard_map/all_gather | solution.py:94
  111.2 2.7 fusion.7
  113.9 3.5 fusion.6
  117.4 3.0 copy.40
  121.1 1.7 copy.44
  122.7 2.3 fusion.13
  125.0 16.5 %fusion.3 = f32[8,64,1,512]{3,2,1,0:T(1,128)S(1)} fusion(f32[8,64,16,1]{2,3,1,0:T(1,128)S(1)} %copy-done.2, f32[8,64,16,512]{3,1,0,2:T(8,128)S(1)} %bitcast.73), kind=kOutput, calls=%fused_computation.13 | convolution fusion | flops 50331648 | bytes 17858560 | tf_op jit(solution)/shard_map/rhp,rhpl->rhl/dot_general | solution.py:54
  144.6 42.2 %all-gather.1 = f32[256,64]{1,0:T(8,128)S(1)} all-gather(f32[8,64]{1,0:T(8,128)S(1)} %get-tuple-element.215), channel_id=3, replica_groups=mesh['pool'=16,'tp'=32] {'tp'}, dimensions={0}, use_global_device_ids=true | all-gather | bytes 67584 | tf_op jit(solution)/shard_map/all_gather | solution.py:11
  186.9 42.8 %all-gather = f32[256,64]{1,0:T(8,128)S(1)} all-gather(f32[8,64]{1,0:T(8,128)S(1)} %get-tuple-element.189), channel_id=2, replica_groups=mesh['pool'=16,'tp'=32] {'tp'}, dimensions={0}, use_global_device_ids=true | all-gather | bytes 67584 | tf_op jit(solution)/shard_map/all_gather | solution.py:11
  229.6 122.5 %all-gather.5.cloned.1.call-done = f32[256,64,512]{2,1,0:T(8,128)} async-done(((f32[8,64,512]{2,1,0:T(8,128)}), f32[256,64,512]{2,1,0:T(8,128)}) %all-gather.5.cloned.1.call-update) | async-done | bytes 33554448 | tf_op jit(solution)/shard_map/all_gather | solution.py:11
  353.4 48.9 %while.19 = (s32[]{:T(128)}, f32[8,64]{1,0:T(8,128)S(1)}, f32[8,64]{1,0:T(8,128)S(1)}, f32[8,64,512]{2,1,0:T(8,128)S(1)}, f32[32,8,64]{2,1,0:T(8,128)S(1)}, /*in...) while((s32[]{:T(128)}, f32[8,64]{1,0:T(8,128)S(1)}, ...), condition=%wide.region_12.13_spmd, body=%wide.region_11.12_spmd.sunk | while | flops 789509 | bytes 3166359 | solution.py:17
  353.5 1.5 fusion.48
  355.1 1.5 fusion.48
  356.6 1.5 fusion.48
  358.2 1.5 fusion.48
  359.8 1.5 fusion.48
  361.4 1.5 fusion.48
  362.9 1.5 fusion.48
  364.5 1.5 fusion.48
  366.1 1.5 fusion.48
  367.7 1.5 fusion.48
  369.3 1.5 fusion.48
  370.8 1.5 fusion.48
  372.4 1.5 fusion.48
  374.0 1.5 fusion.48
  375.6 1.5 fusion.48
  377.1 1.5 fusion.48
  378.7 1.5 fusion.48
  380.3 1.5 fusion.48
  381.9 1.5 fusion.48
  383.4 1.5 fusion.48
  385.0 1.5 fusion.48
  386.6 1.5 fusion.48
  388.2 1.5 fusion.48
  389.8 1.5 fusion.48
  391.3 1.5 fusion.48
  392.9 1.5 fusion.48
  394.5 1.5 fusion.48
  396.1 1.5 fusion.48
  397.6 1.5 fusion.48
  399.2 1.5 fusion.48
  400.8 1.5 fusion.48
  404.3 25.7 %all_gather.31 = bf16[128,256]{1,0:T(8,128)(2,1)S(1)} all-gather(bf16[8,256]{1,0:T(8,128)(2,1)S(1)} %fusion.12), channel_id=1, replica_groups=mesh['pool'=16,'tp'=32] {'pool'}, dimensions={0}, use_global_device_ids=true | all-gather | bytes 69632 | tf_op jit(solution)/shard_map/all_gather | solution.py:109
  431.1 140.2 %all-reduce.2 = bf16[128,448]{1,0:T(8,128)(2,1)S(1)} all-reduce(f32[128,448]{1,0:T(8,128)S(1)} %fusion.38), channel_id=5, replica_groups=mesh['pool'=16,'tp'=32] {'tp'}, use_global_device_ids=true, to_apply=%region_13.14.clone | all-reduce | flops 57344 | bytes 344064
  (100 shorter events, 16.9 us)
Async XLA Ops:
  6.5 40.2 %copy-start = (bf16[16,64,576]{2,1,0:T(8,128)(2,1)S(1)}, bf16[16,64,576]{2,1,0:T(8,128)(2,1)}, u32[]{:S(2)}) copy-start(bf16[16,64,576]{2,1,0:T(8,128)(2,1)} %param.8) | copy-start | bytes 3538948
  41.7 2.2 copy-start.4
  44.0 14.4 %copy-start.3 = (bf16[8,2,576]{2,1,0:T(2,128)(2,1)S(1)}, bf16[8,2,576]{2,1,0:T(2,128)(2,1)}, u32[]{:S(2)}) copy-start(bf16[8,2,576]{2,1,0:T(2,128)(2,1)} %param.11) | copy-start | bytes 55300
  48.8 62.4 %all-to-all-start = ((bf16[16,64,576]{2,1,0:T(8,128)(2,1)}), bf16[16,64,576]{2,1,0:T(8,128)(2,1)S(1)}, u32[]{:S(2)}, u32[]{:S(2)}) async-start(bf16[16,64,576]{2,1,0:T(8,128)(2,1)} %broadcast_select_fusion), calls=%async_computation | async-start | bytes 2621440 | tf_op jit(solution)/shard_map/all_to_all | solution.py:79
  58.4 293.7 %all-gather.5.cloned.1.call-start = ((), (), s32[]{:S(2)}) async-start(), calls=%async_computation.1 | async-start | bytes 34603008 | tf_op jit(solution)/shard_map/all_gather | solution.py:11
  122.7 2.3 copy-start.2
  402.3 169.6 %copy-start.1 = (bf16[16,64,576]{2,1,0:T(8,128)(2,1)S(1)}, bf16[16,64,576]{2,1,0:T(8,128)(2,1)}, u32[]{:S(2)}) copy-start(bf16[16,64,576]{2,1,0:T(8,128)(2,1)} %param.8) | copy-start | bytes 3538948
Sparse Core Ops, SparseCore 0:
  142.8 209.2 all-gather.4
where the time goes:
time: 585 us; the launch traced here: 579 us
  blocking collectives  303 us (52%)
  waiting for transfers between devices  122 us (21%)
  other arithmetic  56.9 us (10%)
  local copies, waits for them, and re-layouts  47.2 us (8%)
  matrix products  23.8 us (4%)
  between operations  14.3 us (2%)
  starting transfers between devices  9.6 us (2%)
    unnamed x1, blocking collectives  140 us
    all_gather x1, waiting for transfers between devices, joined(): everything = jax.tree.map(lambda part: lax.all_gather(part, axis), array)  122 us
    all_gather x2, blocking collectives, joined(): everything = jax.tree.map(lambda part: lax.all_gather(part, axis), array)  85 us
    all_gather x1, blocking collectives, per_device(): all_queries = lax.all_gather(absorbed_query, 'tp', axis=1, tiled=True)  52.5 us
    add x31, other arithmetic, combine_parts(): left_part[2] * left_factor[..., None]  47.3 us
    scatter x1, local copies, waits for them, and re-layouts, per_device(): slot_owner = jnp.zeros((flat_table.shape[0],), jnp.int32).at[flat_table]....  30.5 us
    all_gather x1, blocking collectives, per_device(): all_requests = lax.all_gather(head_output, 'pool', axis=0, tiled=True)  25.7 us
    dot_general x1, matrix products, dense_partials(): jnp.einsum('rhp,rhpl->rhl', factor, page_mixed, precision=lax.Precision.H...  16.5 us
  transfers between devices with their start and end apart: 2, of which 1 were waited for; matrix products, arithmetic and copies ran while one was open for 0% of the time, Pallas kernels for 0%

commit v1 on v0

v1 whole, which is shorter than its diff:
```python
import functools
import itertools

import jax
import jax.numpy as jnp
from jax import lax
from jax.experimental import pallas as pl
from jax.experimental.pallas import tpu as pltpu
from jax.sharding import PartitionSpec as P

MESH = pl.DeviceIdType.MESH
score_scale = 192.0 ** (-0.5)
masked_score = -1e30
F32 = jnp.float32
BF16 = jnp.bfloat16
LANES = 128
MSG = 16
CHUNK = 4
FAR = 3
SITE = 8
PIECES = 1
X_CORE = [(2, 1), (2, 0), (1, 1), (3, 1), (1, 0), (3, 0), (0, 1)]
Z_HI = [2, 1, 3]
TP = [(dz, dx, dc) for dz in (2, 1, 3, 0) for dx in (2, 1, 3, 0) for dc in (1, 0)][:-1]
POOL = [(dz, dy) for dy in (4, 3, 5, 2, 6, 1, 7) for dz in (1, 0)] + [(1, 0)]
SITES = [(dz, dy) for dz, dy in POOL if dy not in (3, 4, 5)]
QUARTERS = 4
GROUPS = 8
BLOCKS = 5


def split3(x):
    hi = x.astype(BF16).astype(F32)
    mid = (x - hi).astype(BF16).astype(F32)
    return hi, mid, x - hi - mid


def each(first, last, body):
    def step(i, carry):
        body(i)
        return carry

    lax.fori_loop(first, last, step, 0)


def kernel(
    n_pool,
    n_tp,
    table_hbm,
    len_hbm,
    store_hbm,
    query_hbm,
    up_hbm,
    proj_hbm,
    out_ref,
    table_ref,
    len_ref,
    store_ref,
    query_ref,
    up_ref,
    proj_ref,
    local_sem,
    stage,
    land,
    q_msg,
    q_land,
    q_part,
    q_all,
    far_msg,
    far_land,
    part_msg,
    part_land,
    head_msg,
    head_land,
    last_msg,
    wide,
    top_ref,
    total_ref,
    mixed_ref,
    page_send,
    page_recv,
    q_send,
    q_recv,
    all_send,
    all_recv,
    part_send,
    part_recv,
    head_send,
    head_recv,
    last_send,
    last_recv,
):
    pool = lax.axis_index("pool")
    tp = lax.axis_index("tp")
    n_y = n_pool // 2
    z, y = pool // n_y, pool % n_y
    sign = 1 - 2 * z
    page_tokens = store_ref.shape[1]
    requests = query_ref.shape[0]
    request, quarter = tp // QUARTERS, tp % QUARTERS
    x, z_hi, core = tp // 8, tp // 2 % 4, tp % 2
    first_page = quarter * n_pool

    def place(at_z, at_y):
        return at_z * n_y + (at_y + 2 * n_y) % n_y

    def across(step):
        dx, dc = step
        return (x + dx) % 4 * 2 + (core + dc) % 2

    def along(dz):
        return (z_hi + dz) % 4

    def tp_of(step):
        dz, dx, dc = step
        return (x + dx) % 4 * 8 + (z_hi + dz) % 4 * 2 + (core + dc) % 2

    def pool_of(step):
        dz, dy = step
        return (z + dz) % 2 * n_y + (y + dy) % n_y

    def number(step):
        return step[0] * 8 + (step[1] if len(step) == 2 else step[1] * 2 + step[2])

    def to(tp_index, pool_index=pool):
        return {"pool": pool_index, "tp": tp_index}

    barrier = pltpu.get_barrier_semaphore()
    loads = [
        pltpu.make_async_copy(source, target, local_sem.at[i])
        for i, (source, target) in enumerate(
            [
                (query_hbm, query_ref),
                (table_hbm.at[pl.ds(pl.multiple_of(first_page, 8), n_pool)], table_ref),
                (store_hbm, store_ref),
                (len_hbm, len_ref),
                (up_hbm, up_ref),
                (proj_hbm, proj_ref),
            ]
        )
    ]
    for load in loads[:3]:
        load.start()

    def greet(tp_index, pool_index=pool):
        device = to(tp_index, pool_index)
        pl.semaphore_signal(barrier, inc=1, device_id=device, device_id_type=MESH)

    for step in X_CORE:
        greet(tp_of((0, *step)))
    for step in SITES:
        greet(tp, pool_of(step))
    for ahead in (FAR, -FAR):
        for dz in Z_HI + [0]:
            greet(tp_of((dz, 0, 0)), place(z, y + ahead))
    for dz in Z_HI:
        greet(tp_of((dz, 0, 0)))
    greetings = len(X_CORE) + len(SITES) + 2 * QUARTERS + len(Z_HI)
    for load in loads[3:]:
        load.start()

    me = pool * n_tp + tp

    def slot_of(group):
        row = group * requests + request

        def look(k, found):
            entry = table_ref[k, row]
            return found + jnp.where(entry >> 4 == me, entry & 15, 0)

        return lax.fori_loop(0, n_pool, look, 0, unroll=True)

    half = page_tokens // 2

    def packed(target, slot):
        for c in range(4):
            target[c * page_tokens : (c + 1) * page_tokens] = store_ref[
                slot, :, c * LANES : (c + 1) * LANES
            ]
        rest = store_ref[slot, :, 4 * LANES :]
        target[4 * page_tokens :] = jnp.concatenate([rest[:half], rest[half:]], axis=1)

    def remote(source, target, sems, i, device):
        send, recv = sems
        return pltpu.make_async_remote_copy(
            src_ref=source,
            dst_ref=target,
            send_sem=send.at[i],
            recv_sem=recv.at[i],
            device_id=device,
            device_id_type=MESH,
        )

    def start(copies):
        for copy in copies:
            copy.start()

    def arrive(copies):
        for copy in copies:
            copy.wait_recv()

    def route(n):
        k = n % 4
        return 1 - n // 4, (6 + k + n // 4 * (k // 2) * (6 * k - 11)) % n_y

    piece_rows = stage.shape[1] // PIECES

    def page_copy(role, n, rows=slice(None)):
        dz, move = route(n)
        to_z = (z + dz) % 2
        direction = (1 - 2 * to_z) * (1 - 2 * role)
        return remote(
            stage.at[role * SITE + n, rows],
            land.at[role * SITE + n, rows],
            (page_send, page_recv),
            role * SITE + n,
            to(tp, to_z * n_y + (y + direction * move + n_y) % n_y),
        )

    def send_pages(role, first, last):
        def send(i):
            n = (i + core * (SITE // 2)) % SITE
            dz, move = route(n)
            to_z = (z + dz) % 2
            direction = 1 - 2 * to_z
            ahead = direction * (1 - 2 * role) * move - direction * (1 - role) * FAR
            packed(stage.at[role * SITE + n], slot_of(to_z * n_y + (y + ahead + 2 * n_y) % n_y))

            @pl.when(n < SITE - 1)
            def _():
                for piece in range(PIECES):
                    page_copy(role, n, pl.ds(piece * piece_rows, piece_rows)).start()

        each(first, last, send)
        if last == SITE:
            local = role * SITE + SITE - 1
            land[local] = stage[local]

    loads[0].wait()
    for i in range(requests):
        for c in range(BLOCKS):
            width = min(LANES, query_ref.shape[-1] - c * LANES)
            wide[i * MSG + 2 * c : i * MSG + 2 * c + 2, :width] = query_ref[
                i, :, c * LANES : c * LANES + width
            ].astype(F32)
        wide[i * MSG + 2 * BLOCKS - 2 : (i + 1) * MSG, LANES // 2 :] = jnp.zeros((8, LANES // 2), F32)
        wide[i * MSG + 2 * BLOCKS : (i + 1) * MSG, : LANES // 2] = jnp.zeros((6, LANES // 2), F32)
    q_msg[...] = wide[: requests * MSG].astype(BF16).reshape(q_msg.shape)

    here = x * 2 + core

    def q_copy(step):
        peer = across(step)
        return remote(
            q_msg.at[pl.ds(peer // 2 * 2, 2)],
            q_land.at[here],
            (q_send, q_recv),
            number(step),
            to(tp_of((0, *step))),
        )

    pl.semaphore_wait(barrier, greetings)
    start(map(q_copy, X_CORE))
    loads[1].wait()
    loads[2].wait()
    send_pages(0, 0, SITE // 2)

    q_land[here] = q_msg[pl.ds(x * 2, 2)]
    arrive(map(q_copy, X_CORE))
    wide[: 2 * SITE * MSG] = q_land[...].reshape(2 * SITE * MSG, LANES).astype(F32)
    for i, c in itertools.product(range(2), range(BLOCKS)):
        halves = [wide[pl.ds(i * MSG + 2 * c + e, SITE, stride=2 * MSG), :] for e in range(2)]
        q_part[i, c] = jnp.concatenate(halves, axis=0).astype(BF16)

    def query_copy(role, dz):
        return remote(
            q_part.at[along(dz) // 2],
            q_all.at[role, z_hi],
            (all_send, all_recv),
            role * QUARTERS + dz,
            to(tp_of((dz, 0, 0)), z * n_y + (y + (1 - role) * sign * FAR + n_y) % n_y),
        )

    def part_copy(step):
        peer = tp_of(step)
        held = along(step[0]) * 8 + across(step[1:])
        return remote(
            part_msg.at[held], part_land.at[tp], (part_send, part_recv), number(step), to(peer)
        )

    def back_copy(rows=slice(None)):
        return remote(
            far_msg.at[rows], far_land.at[rows], (all_send, all_recv), 2 * QUARTERS, to(tp, place(z, y - sign * FAR))
        )

    start([query_copy(0, dz) for dz in Z_HI + [0]])
    start([query_copy(1, dz) for dz in Z_HI])
    q_all[1, z_hi] = q_part[z_hi // 2]
    send_pages(0, SITE // 2, SITE)
    send_pages(1, 0, SITE)
    for load in loads[3:]:
        load.wait()

    lat = up_ref.shape[1]
    heads = 2 * n_tp
    transposed = (((1,), (1,)), ((), ()))

    tokens = CHUNK * page_tokens

    def attend(step):
        role, part = step // 2, (step + core) % 2
        group = z * n_y + (y - sign * (1 - role) * FAR + n_y) % n_y
        row = group * requests + request
        length = len_ref[row]

        @pl.when(step % 2 == 0)
        def _():
            top_ref[...] = jnp.full(top_ref.shape, masked_score, F32)
            total_ref[...] = jnp.zeros(total_ref.shape, F32)
            mixed_ref[...] = jnp.zeros(mixed_ref.shape, F32)
            arrive([query_copy(role, dz) for dz in Z_HI])

            @pl.when(role == 0)
            def _():
                query_copy(0, 0).wait_recv()

        lane = lax.broadcasted_iota(jnp.int32, (1, tokens), 1)
        n = part * CHUNK + lane % (CHUNK * half) // half
        dz, move = route(n)
        source = (z + dz) % 2 * n_y + (y - sign * (1 - 2 * role) * move + n_y) % n_y
        limit = jnp.zeros_like(lane)
        for k in range(n_pool):
            holder = table_ref[k, row] >> 9
            limit = jnp.where(source == holder, length - (first_page + k) * page_tokens, limit)
        live = lane // (CHUNK * half) * half + lane % half < limit

        blocks = [
            jnp.concatenate([q_all[role, u, c] for u in range(QUARTERS)], axis=0)
            for c in range(BLOCKS)
        ]
        query = jnp.concatenate(blocks[:4], axis=1)
        rest = blocks[4][:, : LANES // 2]
        blank = jnp.zeros_like(rest)
        rest = jnp.concatenate(
            [jnp.concatenate([rest, blank], axis=1), jnp.concatenate([blank, rest], axis=1)], axis=0
        )
        first = part * CHUNK
        each(first, first + CHUNK - part, lambda n: page_copy(role, n).wait_recv())
        block = land[pl.ds(role * SITE + first, CHUNK)]

        def rows(begin):
            return block[:, begin : begin + half].reshape(CHUNK * half, LANES)

        keys = jnp.concatenate(
            [
                jnp.concatenate([rows(c * page_tokens + h * half) for c in range(4)], axis=1)
                for h in range(2)
            ],
            axis=0,
        )
        scores = lax.dot_general(query, keys, transposed, preferred_element_type=F32)
        extra = lax.dot_general(rest, rows(4 * page_tokens), transposed, preferred_element_type=F32)
        scores += jnp.concatenate([extra[:heads], extra[heads:]], axis=1)
        scores = jnp.where(live, scores * score_scale, masked_score)
        top = top_ref[...]
        new_top = jnp.maximum(top, jnp.max(scores, axis=1, keepdims=True))
        weights = jnp.where(live, jnp.exp(scores - new_top[:, :1]), 0.0)
        scale = jnp.exp(top - new_top)
        total = total_ref[...] * scale + jnp.sum(weights, axis=1, keepdims=True)
        update = jnp.dot(weights.astype(BF16), keys, preferred_element_type=F32)
        mixed = mixed_ref[...] * scale[:, :1] + update
        top_ref[...] = new_top
        total_ref[...] = total
        mixed_ref[...] = mixed

        @pl.when(step == 1)
        def _():
            lse, even = normalised(new_top, total, mixed)
            for c in range(4):
                far_msg[c * heads : (c + 1) * heads] = even[:, c * LANES : (c + 1) * LANES].astype(BF16)
            lane = lax.broadcasted_iota(jnp.int32, (heads, LANES), 1)
            hi, mid, low = split3(lse)
            stat = jnp.where(lane == 0, hi, jnp.where(lane == 1, mid, jnp.where(lane == 2, low, 0.0)))
            far_msg[4 * heads :] = stat.astype(BF16)
            start([back_copy(pl.ds(c * heads, heads)) for c in range(BLOCKS)])

    def normalised(top, total, mixed):
        some = total > 0.0
        safe = jnp.where(some, total, 1.0)
        inverse = 1.0 / safe
        return jnp.where(some, top + jnp.log(safe), masked_score), mixed * inverse[:, :1]

    each(0, 4, attend)
    back_copy().wait_recv()
    back = jnp.sum(far_land[4 * heads :].astype(F32), axis=1, keepdims=True)
    top = top_ref[...]
    new_top = jnp.maximum(top, back)
    scale = jnp.exp(top - new_top)
    share = jnp.where(back > 0.5 * masked_score, jnp.exp(back - new_top), 0.0)
    mixed = jnp.concatenate(
        [
            mixed_ref[:, c * LANES : (c + 1) * LANES] * scale
            + far_land[c * heads : (c + 1) * heads].astype(F32) * share
            for c in range(4)
        ],
        axis=1,
    )
    lse, even = normalised(new_top, total_ref[...] * scale + share, mixed)
    parts = split3(lse) + (jnp.zeros_like(lse),)
    for u, e in itertools.product(range(QUARTERS), range(2)):
        mine = slice(u * MSG + e * 8, u * MSG + e * 8 + 8)
        for c in range(4):
            row = u * 8 * MSG + 2 * c + e
            wide[pl.ds(row, 8, stride=MSG), :] = even[mine, c * LANES : (c + 1) * LANES]
            wide[pl.ds(row + 8, 8, stride=MSG), :] = parts[c][mine]
    part_msg[...] = wide[...].astype(BF16).reshape(part_msg.shape)
    part_copies = [part_copy(step) for step in TP]
    start(part_copies)
    part_land[tp] = part_msg[z_hi * 8 + here]
    arrive(part_copies)

    wide[...] = part_land[...].reshape(wide.shape).astype(F32)
    values = []
    for e in range(2):

        def rows(k, j):
            return wide[pl.ds(k * MSG + 2 * j + e, GROUPS, stride=QUARTERS * MSG), :]

        lses = [rows(k, 4) + rows(k, 5) + rows(k, 6) for k in range(QUARTERS)]
        best = functools.reduce(jnp.maximum, lses)
        share = [jnp.exp(one - best) for one in lses]
        norm = 1.0 / functools.reduce(jnp.add, share)
        attended = []
        for c in range(4):
            block = functools.reduce(jnp.add, [share[k] * rows(k, c) for k in range(QUARTERS)])
            attended.append((block * norm).astype(BF16))
        attended = jnp.concatenate(attended, axis=1)
        values.append(jnp.dot(attended, up_ref[e], preferred_element_type=F32))
    head_msg[...] = jnp.concatenate(values, axis=0).astype(BF16)

    def head_copy(step):
        return remote(
            head_msg, head_land.at[pool], (head_send, head_recv), number(step), to(tp, pool_of(step))
        )

    start(map(head_copy, POOL))
    head_land[pool] = head_msg[...]
    arrive(map(head_copy, POOL))

    landed = head_land[...].astype(F32)
    left = [landed[:, 8 * e : 8 * e + 8].reshape(4 * n_tp, LANES).astype(BF16) for e in range(2)]
    product = lax.dot_general(
        jnp.concatenate(left, axis=1), proj_ref[...], transposed, preferred_element_type=F32
    )
    columns = proj_ref.shape[0]
    blank = jnp.zeros((4 * n_tp, 4 * LANES - columns), F32)
    product = jnp.concatenate([product, blank], axis=1)
    for j in range(n_tp):
        last_msg[j] = product[4 * j : 4 * j + 4].astype(BF16)

    def last_copy(step):
        peer = tp_of(step)
        return remote(
            last_msg.at[peer], out_ref.at[tp], (last_send, last_recv), number(step), to(peer)
        )

    start(map(last_copy, TP))
    own = pltpu.make_async_copy(last_msg.at[tp], out_ref.at[tp], last_send.at[0])
    own.start()
    each(0, SITE - 1, lambda n: page_copy(0, n).wait_send())
    each(0, SITE - 1, lambda n: page_copy(1, n).wait_send())
    sent = [q_copy(step) for step in X_CORE]
    sent += [query_copy(0, dz) for dz in Z_HI + [0]] + [query_copy(1, dz) for dz in Z_HI]
    sent += [back_copy()] + part_copies
    sent += [head_copy(step) for step in POOL]
    sent += [last_copy(step) for step in TP]
    for copy in sent:
        copy.wait_send()
    own.wait()
    arrive(map(last_copy, TP))


def per_device(n_pool, n_tp, page_store, page_table, context_len, absorbed_query, value_up, out_proj):
    pages, tokens, key_width = page_store.shape
    requests = absorbed_query.shape[0]
    columns = out_proj.shape[1]
    hbm = pl.BlockSpec(memory_space=pltpu.HBM)
    message = lambda *lead: pltpu.VMEM((*lead, MSG, LANES), BF16)
    sems = lambda n: [pltpu.SemaphoreType.DMA((n,)), pltpu.SemaphoreType.DMA((n,))]
    summands = pl.pallas_call(
        functools.partial(kernel, n_pool, n_tp),
        out_shape=jax.ShapeDtypeStruct((n_tp, 4, 4 * LANES), BF16),
        in_specs=[hbm] * 6,
        out_specs=hbm,
        scratch_shapes=[
            pltpu.SMEM((n_pool, page_table.shape[0]), jnp.int32),
            pltpu.SMEM(context_len.shape, jnp.int32),
            pltpu.VMEM(page_store.shape, BF16),
            pltpu.VMEM(absorbed_query.shape, BF16),
            pltpu.VMEM(value_up.shape, BF16),
            pltpu.VMEM(out_proj.shape[::-1], BF16),
            pltpu.SemaphoreType.DMA((6,)),
            pltpu.VMEM((n_pool, tokens * key_width // LANES, LANES), BF16),
            pltpu.VMEM((n_pool, tokens * key_width // LANES, LANES), BF16),
            message(GROUPS),
            message(SITE, 2),
            message(2, BLOCKS),
            message(2, QUARTERS, BLOCKS),
            pltpu.VMEM((BLOCKS * 2 * n_tp, LANES), BF16),
            pltpu.VMEM((BLOCKS * 2 * n_tp, LANES), BF16),
            message(n_tp),
            message(n_tp),
            message(),
            message(n_pool),
            pltpu.VMEM((n_tp, 4, 4 * LANES), BF16),
            pltpu.VMEM((n_tp * MSG, LANES), F32),
            pltpu.VMEM((2 * n_tp, LANES), F32),
            pltpu.VMEM((2 * n_tp, LANES), F32),
            pltpu.VMEM((2 * n_tp, value_up.shape[1]), F32),
            *sems(2 * SITE),
            *sems(4 * SITE),
            *sems(2 * QUARTERS + 1),
            *sems(n_tp),
            *sems(2 * SITE),
            *sems(n_tp),
        ],
        compiler_params=pltpu.CompilerParams(
            collective_id=0, has_side_effects=True, vmem_limit_bytes=62 * 1024 * 1024
        ),
        name="mla_decode",
    )(page_table.T, context_len, page_store, absorbed_query, value_up, out_proj.T)
    return jnp.sum(summands.astype(F32), axis=0)[:, :columns].astype(BF16)


def solution(mesh):
    placed = (
        P(("pool", "tp"), None, None),
        P(),
        P(),
        P("pool", "tp", None),
        P("tp", None, None),
        P("tp", "pool"),
    )
    return jax.shard_map(
        functools.partial(per_device, mesh.shape["pool"], mesh.shape["tp"]),
        mesh=mesh,
        in_specs=placed,
        out_specs=P("tp", "pool"),
        check_vma=False,
    )
```

time: 585 us -> 62.5 us (0.11); the launches traced: 579 us -> 62.4 us
  blocking collectives: 303 us -> 0 us
  waiting for transfers between devices: 122 us -> 0 us
  Pallas kernels: 0 us -> 60.8 us
  other arithmetic: 56.9 us -> 1.57 us
  local copies, waits for them, and re-layouts: 47.2 us -> 0 us
  matrix products: 23.8 us -> 0 us
  between operations: 14.3 us -> 0.01 us
  starting transfers between devices: 9.6 us -> 0 us
    all_gather x4 -> x0, blocking collectives: 163 us -> none  [the longest x2 85 us: joined(): everything = jax.tree.map(lambda part: lax.all_gather(part, axis), array)]
    unnamed x1 -> x0, blocking collectives: 140 us -> none
    all_gather x1 -> x0, waiting for transfers between devices: 122 us -> none  [joined(): everything = jax.tree.map(lambda part: lax.all_gather(part, axis), array)]
    pallas_call x0 -> x1, Pallas kernels: none -> 60.8 us  [per_device(): pl.pallas_call(functools.partial(kernel, n_pool, n_tp), out_shape=jax.Sha...]
    add x64 -> x0, other arithmetic: 48 us -> none  [the longest x31 47.3 us: combine_parts(): left_part[2] * left_factor[..., None]]
    scatter x1 -> x0, local copies, waits for them, and re-layouts: 30.5 us -> none  [per_device(): slot_owner = jnp.zeros((flat_table.shape[0],), jnp.int32).at[flat_table]....]
    dot_general x4 -> x0, matrix products: 21.5 us -> none  [the longest x1 16.5 us: dense_partials(): jnp.einsum('rhp,rhpl->rhl', factor, page_mixed, precision=lax.Precision.H...]
    all_to_all x1 -> x0, starting transfers between devices: 9.56 us -> none  [per_device(): lax.all_to_all(outgoing, 'pool', split_axis=0, concat_axis=0, tiled=True)]
  transfers between devices with their start and end apart: 2 -> 0, of which waited for: 1 -> 0; matrix products, arithmetic and copies ran while one was open for 0% -> 0% of each run, Pallas kernels for 0% -> 0%
where the time goes in v1:
time: 62.5 us; the launch traced here: 62.4 us
  Pallas kernels  60.8 us (97%)
  other arithmetic  1.57 us (3%)
    pallas_call x1, Pallas kernels, per_device(): pl.pallas_call(functools.partial(kernel, n_pool, n_tp), out_shape=jax.Sha...  60.8 us
    reduce_sum x1, other arithmetic, per_device(): return jnp.sum(summands.astype(F32), axis=0)[:, :columns].astype(BF16)  1.57 us

profile of v1, /device:TPU:1, one launch (start us, length us, event | category | flops | bytes accessed | tf_op | source)
XLA Modules:
  0.0 62.4 jit_solution(12868712072326918840)
XLA Ops:
  0.0 60.8 %mla_decode.1 = bf16[32,4,512]{2,1,0:T(4,128)(2,1)} custom-call(s32[64,128]{1,0:T(8,128)} %bitcast.4, s32[128]{0:T(128)} %len_hbm.1, bf16[16,64,576]{2,1,0:T(8,128)(2,1)} %store_hbm.1, bf16[8,2,576]{2,1,0:T(2,128)(2,1)} %query_hbm.1, bf16[2,512,128]{2,1,0:T(8,128)(2,1)} %up_hbm.1, bf16[448,256]{1,0:T(8,128)(2,1)} %bitcast.3), custom_call_target="tpu_custom_call" | custom-call | tf_op jit(solution)/shard_map/mla_decode/pallas_call | solution.py:490
  60.8 1.6 %reduce = bf16[4,512]{1,0:T(4,128)(2,1)} reduce(bf16[32,4,512]{2,1,0:T(4,128)(2,1)} %mla_decode.1, bf16[]{:T(256)} %constant.5), dimensions={0}, to_apply=%region_0.0.clone | reduce | flops 63488 | bytes 135170 | tf_op jit(solution)/shard_map/reduce_sum | solution.py:532

commit v2 on v1

--- a/solution.py
+++ b/solution.py
@@ -19,6 +19,7 @@
 FAR = 3
 SITE = 8
 PIECES = 1
+SELF = (0, 0, 0)
 X_CORE = [(2, 1), (2, 0), (1, 1), (3, 1), (1, 0), (3, 0), (0, 1)]
 Z_HI = [2, 1, 3]
 TP = [(dz, dx, dc) for dz in (2, 1, 3, 0) for dx in (2, 1, 3, 0) for dc in (1, 0)][:-1]
@@ -66,8 +67,6 @@
     q_land,
     q_part,
     q_all,
-    far_msg,
-    far_land,
     part_msg,
     part_land,
     head_msg,
@@ -281,16 +280,15 @@
             to(tp_of((dz, 0, 0)), z * n_y + (y + (1 - role) * sign * FAR + n_y) % n_y),
         )
 
-    def part_copy(step):
+    def part_copy(role, step):
         peer = tp_of(step)
         held = along(step[0]) * 8 + across(step[1:])
         return remote(
-            part_msg.at[held], part_land.at[tp], (part_send, part_recv), number(step), to(peer)
-        )
-
-    def back_copy(rows=slice(None)):
-        return remote(
-            far_msg.at[rows], far_land.at[rows], (all_send, all_recv), 2 * QUARTERS, to(tp, place(z, y - sign * FAR))
+            part_msg.at[role, held],
+            part_land.at[role, tp],
+            (part_send, part_recv),
+            role * n_tp + number(step),
+            to(peer, z * n_y + (y - (1 - role) * sign * FAR + n_y) % n_y),
         )
 
     start([query_copy(0, dz) for dz in Z_HI + [0]])
@@ -373,50 +371,31 @@
         total_ref[...] = total
         mixed_ref[...] = mixed
 
-        @pl.when(step == 1)
+        @pl.when(step % 2 == 1)
         def _():
-            lse, even = normalised(new_top, total, mixed)
-            for c in range(4):
-                far_msg[c * heads : (c + 1) * heads] = even[:, c * LANES : (c + 1) * LANES].astype(BF16)
-            lane = lax.broadcasted_iota(jnp.int32, (heads, LANES), 1)
-            hi, mid, low = split3(lse)
-            stat = jnp.where(lane == 0, hi, jnp.where(lane == 1, mid, jnp.where(lane == 2, low, 0.0)))
-            far_msg[4 * heads :] = stat.astype(BF16)
-            start([back_copy(pl.ds(c * heads, heads)) for c in range(BLOCKS)])
-
-    def normalised(top, total, mixed):
-        some = total > 0.0
-        safe = jnp.where(some, total, 1.0)
-        inverse = 1.0 / safe
-        return jnp.where(some, top + jnp.log(safe), masked_score), mixed * inverse[:, :1]
+            some = total > 0.0
+            safe = jnp.where(some, total, 1.0)
+            inverse = 1.0 / safe
+            even = mixed * inverse[:, :1]
+            parts = split3(jnp.where(some, new_top + jnp.log(safe), masked_score))
+            parts += (jnp.zeros_like(total),)
+            for u, e in itertools.product(range(QUARTERS), range(2)):
+                mine = slice(u * MSG + e * 8, u * MSG + e * 8 + 8)
+                for c in range(4):
+                    row = u * 8 * MSG + 2 * c + e
+                    wide[pl.ds(row, 8, stride=MSG), :] = even[mine, c * LANES : (c + 1) * LANES]
+                    wide[pl.ds(row + 8, 8, stride=MSG), :] = parts[c][mine]
+            part_msg[role] = wide[: n_tp * MSG].astype(BF16).reshape(n_tp, MSG, LANES)
+            start([part_copy(role, step) for step in TP])
+
+            @pl.when(role == 0)
+            def _():
+                part_copy(0, SELF).start()
 
     each(0, 4, attend)
-    back_copy().wait_recv()
-    back = jnp.sum(far_land[4 * heads :].astype(F32), axis=1, keepdims=True)
-    top = top_ref[...]
-    new_top = jnp.maximum(top, back)
-    scale = jnp.exp(top - new_top)
-    share = jnp.where(back > 0.5 * masked_score, jnp.exp(back - new_top), 0.0)
-    mixed = jnp.concatenate(
-        [
-            mixed_ref[:, c * LANES : (c + 1) * LANES] * scale
-            + far_land[c * heads : (c + 1) * heads].astype(F32) * share
-            for c in range(4)
-        ],
-        axis=1,
-    )
-    lse, even = normalised(new_top, total_ref[...] * scale + share, mixed)
-    parts = split3(lse) + (jnp.zeros_like(lse),)
-    for u, e in itertools.product(range(QUARTERS), range(2)):
-        mine = slice(u * MSG + e * 8, u * MSG + e * 8 + 8)
-        for c in range(4):
-            row = u * 8 * MSG + 2 * c + e
-            wide[pl.ds(row, 8, stride=MSG), :] = even[mine, c * LANES : (c + 1) * LANES]
-            wide[pl.ds(row + 8, 8, stride=MSG), :] = parts[c][mine]
-    part_msg[...] = wide[...].astype(BF16).reshape(part_msg.shape)
-    part_copies = [part_copy(step) for step in TP]
-    start(part_copies)
-    part_land[tp] = part_msg[z_hi * 8 + here]
+    part_land[1, tp] = part_msg[1, z_hi * 8 + here]
+    part_copies = [part_copy(0, step) for step in TP + [SELF]]
+    part_copies += [part_copy(1, step) for step in TP]
     arrive(part_copies)
 
     wide[...] = part_land[...].reshape(wide.shape).astype(F32)
@@ -424,15 +403,17 @@
     for e in range(2):
 
         def rows(k, j):
-            return wide[pl.ds(k * MSG + 2 * j + e, GROUPS, stride=QUARTERS * MSG), :]
-
-        lses = [rows(k, 4) + rows(k, 5) + rows(k, 6) for k in range(QUARTERS)]
+            return wide[
+                pl.ds(k // 4 * n_tp * MSG + k % 4 * MSG + 2 * j + e, GROUPS, stride=QUARTERS * MSG), :
+            ]
+
+        lses = [rows(k, 4) + rows(k, 5) + rows(k, 6) for k in range(2 * QUARTERS)]
         best = functools.reduce(jnp.maximum, lses)
         share = [jnp.exp(one - best) for one in lses]
         norm = 1.0 / functools.reduce(jnp.add, share)
         attended = []
         for c in range(4):
-            block = functools.reduce(jnp.add, [share[k] * rows(k, c) for k in range(QUARTERS)])
+            block = functools.reduce(jnp.add, [share[k] * rows(k, c) for k in range(2 * QUARTERS)])
             attended.append((block * norm).astype(BF16))
         attended = jnp.concatenate(attended, axis=1)
         values.append(jnp.dot(attended, up_ref[e], preferred_element_type=F32))
@@ -471,7 +452,7 @@
     each(0, SITE - 1, lambda n: page_copy(1, n).wait_send())
     sent = [q_copy(step) for step in X_CORE]
     sent += [query_copy(0, dz) for dz in Z_HI + [0]] + [query_copy(1, dz) for dz in Z_HI]
-    sent += [back_copy()] + part_copies
+    sent += part_copies
     sent += [head_copy(step) for step in POOL]
     sent += [last_copy(step) for step in TP]
     for copy in sent:
@@ -506,21 +487,19 @@
             message(SITE, 2),
             message(2, BLOCKS),
             message(2, QUARTERS, BLOCKS),
-            pltpu.VMEM((BLOCKS * 2 * n_tp, LANES), BF16),
-            pltpu.VMEM((BLOCKS * 2 * n_tp, LANES), BF16),
-            message(n_tp),
-            message(n_tp),
+            message(2, n_tp),
+            message(2, n_tp),
             message(),
             message(n_pool),
             pltpu.VMEM((n_tp, 4, 4 * LANES), BF16),
-            pltpu.VMEM((n_tp * MSG, LANES), F32),
+            pltpu.VMEM((2 * n_tp * MSG, LANES), F32),
             pltpu.VMEM((2 * n_tp, LANES), F32),
             pltpu.VMEM((2 * n_tp, LANES), F32),
             pltpu.VMEM((2 * n_tp, value_up.shape[1]), F32),
             *sems(2 * SITE),
             *sems(4 * SITE),
-            *sems(2 * QUARTERS + 1),
-            *sems(n_tp),
+            *sems(2 * QUARTERS),
+            *sems(2 * n_tp),
             *sems(2 * SITE),
             *sems(n_tp),
         ],

time: 62.5 us -> 62.4 us (level)
  no operation moved by 1% of the time
where the time goes in v2:
time: 62.4 us; the launch traced here: 62.3 us
  Pallas kernels  60.7 us (97%)
  other arithmetic  1.57 us (3%)
    pallas_call x1, Pallas kernels, per_device(): pl.pallas_call(functools.partial(kernel, n_pool, n_tp), out_shape=jax.Sha...  60.7 us
    reduce_sum x1, other arithmetic, per_device(): return jnp.sum(summands.astype(F32), axis=0)[:, :columns].astype(BF16)  1.57 us

profile of v2, /device:TPU:1, one launch (start us, length us, event | category | flops | bytes accessed | tf_op | source)
XLA Modules:
  0.0 62.3 jit_solution(16209095863822550793)
XLA Ops:
  0.0 60.7 %mla_decode.1 = bf16[32,4,512]{2,1,0:T(4,128)(2,1)} custom-call(s32[64,128]{1,0:T(8,128)} %bitcast.4, s32[128]{0:T(128)} %len_hbm.1, bf16[16,64,576]{2,1,0:T(8,128)(2,1)} %store_hbm.1, bf16[8,2,576]{2,1,0:T(2,128)(2,1)} %query_hbm.1, bf16[2,512,128]{2,1,0:T(8,128)(2,1)} %up_hbm.1, bf16[448,256]{1,0:T(8,128)(2,1)} %bitcast.3), custom_call_target="tpu_custom_call" | custom-call | tf_op jit(solution)/shard_map/mla_decode/pallas_call | solution.py:471
  60.7 1.6 %reduce = bf16[4,512]{1,0:T(4,128)(2,1)} reduce(bf16[32,4,512]{2,1,0:T(4,128)(2,1)} %mla_decode.1, bf16[]{:T(256)} %constant.5), dimensions={0}, to_apply=%region_0.0.clone | reduce | flops 63488 | bytes 135170 | tf_op jit(solution)/shard_map/reduce_sum | solution.py:511

commit v3 on v1

--- a/solution.py
+++ b/solution.py
@@ -18,7 +18,6 @@
 CHUNK = 4
 FAR = 3
 SITE = 8
-PIECES = 1
 X_CORE = [(2, 1), (2, 0), (1, 1), (3, 1), (1, 0), (3, 0), (0, 1)]
 Z_HI = [2, 1, 3]
 TP = [(dz, dx, dc) for dz in (2, 1, 3, 0) for dx in (2, 1, 3, 0) for dc in (1, 0)][:-1]
@@ -74,9 +73,6 @@
     head_land,
     last_msg,
     wide,
-    top_ref,
-    total_ref,
-    mixed_ref,
     page_send,
     page_recv,
     q_send,
@@ -96,7 +92,7 @@
     z, y = pool // n_y, pool % n_y
     sign = 1 - 2 * z
     page_tokens = store_ref.shape[1]
-    requests = query_ref.shape[0]
+    requests = query_hbm.shape[0]
     request, quarter = tp // QUARTERS, tp % QUARTERS
     x, z_hi, core = tp // 8, tp // 2 % 4, tp % 2
     first_page = quarter * n_pool
@@ -130,16 +126,16 @@
         pltpu.make_async_copy(source, target, local_sem.at[i])
         for i, (source, target) in enumerate(
             [
-                (query_hbm, query_ref),
                 (table_hbm.at[pl.ds(pl.multiple_of(first_page, 8), n_pool)], table_ref),
                 (store_hbm, store_ref),
+                (query_hbm, query_ref),
                 (len_hbm, len_ref),
                 (up_hbm, up_ref),
                 (proj_hbm, proj_ref),
             ]
         )
     ]
-    for load in loads[:3]:
+    for load in (loads[2], loads[0], loads[1]):
         load.start()
 
     def greet(tp_index, pool_index=pool):
@@ -203,15 +199,13 @@
         k = n % 4
         return 1 - n // 4, (6 + k + n // 4 * (k // 2) * (6 * k - 11)) % n_y
 
-    piece_rows = stage.shape[1] // PIECES
-
-    def page_copy(role, n, rows=slice(None)):
+    def page_copy(role, n):
         dz, move = route(n)
         to_z = (z + dz) % 2
         direction = (1 - 2 * to_z) * (1 - 2 * role)
         return remote(
-            stage.at[role * SITE + n, rows],
-            land.at[role * SITE + n, rows],
+            stage.at[role * SITE + n],
+            land.at[role * SITE + n],
             (page_send, page_recv),
             role * SITE + n,
             to(tp, to_z * n_y + (y + direction * move + n_y) % n_y),
@@ -228,15 +222,14 @@
 
             @pl.when(n < SITE - 1)
             def _():
-                for piece in range(PIECES):
-                    page_copy(role, n, pl.ds(piece * piece_rows, piece_rows)).start()
+                page_copy(role, n).start()
 
         each(first, last, send)
         if last == SITE:
             local = role * SITE + SITE - 1
             land[local] = stage[local]
 
-    loads[0].wait()
+    loads[2].wait()
     for i in range(requests):
         for c in range(BLOCKS):
             width = min(LANES, query_ref.shape[-1] - c * LANES)
@@ -261,8 +254,8 @@
 
     pl.semaphore_wait(barrier, greetings)
     start(map(q_copy, X_CORE))
+    loads[0].wait()
     loads[1].wait()
-    loads[2].wait()
     send_pages(0, 0, SITE // 2)
 
     q_land[here] = q_msg[pl.ds(x * 2, 2)]
@@ -305,35 +298,23 @@
     heads = 2 * n_tp
     transposed = (((1,), (1,)), ((), ()))
 
-    tokens = CHUNK * page_tokens
-
-    def attend(step):
-        role, part = step // 2, (step + core) % 2
+    def attend(role, first, count, last, before):
         group = z * n_y + (y - sign * (1 - role) * FAR + n_y) % n_y
         row = group * requests + request
         length = len_ref[row]
 
-        @pl.when(step % 2 == 0)
-        def _():
-            top_ref[...] = jnp.full(top_ref.shape, masked_score, F32)
-            total_ref[...] = jnp.zeros(total_ref.shape, F32)
-            mixed_ref[...] = jnp.zeros(mixed_ref.shape, F32)
-            arrive([query_copy(role, dz) for dz in Z_HI])
-
-            @pl.when(role == 0)
-            def _():
-                query_copy(0, 0).wait_recv()
-
-        lane = lax.broadcasted_iota(jnp.int32, (1, tokens), 1)
-        n = part * CHUNK + lane % (CHUNK * half) // half
-        dz, move = route(n)
+        lane = lax.broadcasted_iota(jnp.int32, (1, count * page_tokens), 1)
+        dz, move = route(first + lane % (count * half) // half)
         source = (z + dz) % 2 * n_y + (y - sign * (1 - 2 * role) * move + n_y) % n_y
         limit = jnp.zeros_like(lane)
         for k in range(n_pool):
             holder = table_ref[k, row] >> 9
             limit = jnp.where(source == holder, length - (first_page + k) * page_tokens, limit)
-        live = lane // (CHUNK * half) * half + lane % half < limit
-
+        live = lane // (count * half) * half + lane % half < limit
+
+        each(first, last, lambda n: page_copy(role, n).wait_recv())
+        if before is None:
+            arrive([query_copy(role, dz) for dz in Z_HI + [0] * (1 - role)])
         blocks = [
             jnp.concatenate([q_all[role, u, c] for u in range(QUARTERS)], axis=0)
             for c in range(BLOCKS)
@@ -344,12 +325,10 @@
         rest = jnp.concatenate(
             [jnp.concatenate([rest, blank], axis=1), jnp.concatenate([blank, rest], axis=1)], axis=0
         )
-        first = part * CHUNK
-        each(first, first + CHUNK - part, lambda n: page_copy(role, n).wait_recv())
-        block = land[pl.ds(role * SITE + first, CHUNK)]
+        block = land[pl.ds(role * SITE + first, count)]
 
         def rows(begin):
-            return block[:, begin : begin + half].reshape(CHUNK * half, LANES)
+            return block[:, begin : begin + half].reshape(count * half, LANES)
 
         keys = jnp.concatenate(
             [
@@ -362,27 +341,17 @@
         extra = lax.dot_general(rest, rows(4 * page_tokens), transposed, preferred_element_type=F32)
         scores += jnp.concatenate([extra[:heads], extra[heads:]], axis=1)
         scores = jnp.where(live, scores * score_scale, masked_score)
-        top = top_ref[...]
-        new_top = jnp.maximum(top, jnp.max(scores, axis=1, keepdims=True))
-        weights = jnp.where(live, jnp.exp(scores - new_top[:, :1]), 0.0)
-        scale = jnp.exp(top - new_top)
-        total = total_ref[...] * scale + jnp.sum(weights, axis=1, keepdims=True)
-        update = jnp.dot(weights.astype(BF16), keys, preferred_element_type=F32)
-        mixed = mixed_ref[...] * scale[:, :1] + update
-        top_ref[...] = new_top
-        total_ref[...] = total
-        mixed_ref[...] = mixed
-
-        @pl.when(step == 1)
-        def _():
-            lse, even = normalised(new_top, total, mixed)
-            for c in range(4):
-                far_msg[c * heads : (c + 1) * heads] = even[:, c * LANES : (c + 1) * LANES].astype(BF16)
-            lane = lax.broadcasted_iota(jnp.int32, (heads, LANES), 1)
-            hi, mid, low = split3(lse)
-            stat = jnp.where(lane == 0, hi, jnp.where(lane == 1, mid, jnp.where(lane == 2, low, 0.0)))
-            far_msg[4 * heads :] = stat.astype(BF16)
-            start([back_copy(pl.ds(c * heads, heads)) for c in range(BLOCKS)])
+        top = jnp.broadcast_to(jnp.max(scores, axis=1, keepdims=True), (heads, LANES))
+        if before is not None:
+            top = jnp.maximum(top, before[0])
+        weights = jnp.where(live, jnp.exp(scores - top[:, :1]), 0.0)
+        total = jnp.broadcast_to(jnp.sum(weights, axis=1, keepdims=True), (heads, LANES))
+        mixed = jnp.dot(weights.astype(BF16), keys, preferred_element_type=F32)
+        if before is not None:
+            scale = jnp.exp(before[0] - top)
+            total += before[1] * scale
+            mixed += before[2] * scale[:, :1]
+        return top, total, mixed
 
     def normalised(top, total, mixed):
         some = total > 0.0
@@ -390,22 +359,33 @@
         inverse = 1.0 / safe
         return jnp.where(some, top + jnp.log(safe), masked_score), mixed * inverse[:, :1]
 
-    each(0, 4, attend)
+    first, second = core * CHUNK, (1 - core) * CHUNK
+    state = attend(0, first, CHUNK, first + CHUNK - core, None)
+    lse, even = normalised(*attend(0, second, CHUNK, second + CHUNK - (1 - core), state))
+    for c in range(4):
+        far_msg[c * heads : (c + 1) * heads] = even[:, c * LANES : (c + 1) * LANES].astype(BF16)
+    lane = lax.broadcasted_iota(jnp.int32, (heads, LANES), 1)
+    hi, mid, low = split3(lse)
+    stat = jnp.where(lane == 0, hi, jnp.where(lane == 1, mid, jnp.where(lane == 2, low, 0.0)))
+    far_msg[4 * heads :] = stat.astype(BF16)
+    start([back_copy(pl.ds(c * heads, heads)) for c in range(BLOCKS)])
+
+    state = attend(1, first, CHUNK, first + CHUNK - core, None)
+    top, total, mixed = attend(1, second, CHUNK, second + CHUNK - (1 - core), state)
     back_copy().wait_recv()
     back = jnp.sum(far_land[4 * heads :].astype(F32), axis=1, keepdims=True)
-    top = top_ref[...]
     new_top = jnp.maximum(top, back)
     scale = jnp.exp(top - new_top)
     share = jnp.where(back > 0.5 * masked_score, jnp.exp(back - new_top), 0.0)
     mixed = jnp.concatenate(
         [
-            mixed_ref[:, c * LANES : (c + 1) * LANES] * scale
+            mixed[:, c * LANES : (c + 1) * LANES] * scale
             + far_land[c * heads : (c + 1) * heads].astype(F32) * share
             for c in range(4)
         ],
         axis=1,
     )
-    lse, even = normalised(new_top, total_ref[...] * scale + share, mixed)
+    lse, even = normalised(new_top, total * scale + share, mixed)
     parts = split3(lse) + (jnp.zeros_like(lse),)
     for u, e in itertools.product(range(QUARTERS), range(2)):
         mine = slice(u * MSG + e * 8, u * MSG + e * 8 + 8)
@@ -514,9 +494,6 @@
             message(n_pool),
             pltpu.VMEM((n_tp, 4, 4 * LANES), BF16),
             pltpu.VMEM((n_tp * MSG, LANES), F32),
-            pltpu.VMEM((2 * n_tp, LANES), F32),
-            pltpu.VMEM((2 * n_tp, LANES), F32),
-            pltpu.VMEM((2 * n_tp, value_up.shape[1]), F32),
             *sems(2 * SITE),
             *sems(4 * SITE),
             *sems(2 * QUARTERS + 1),

time: 62.5 us -> 62.5 us (level)
  no operation moved by 1% of the time
where the time goes in v3:
time: 62.5 us; the launch traced here: 62.3 us
  Pallas kernels  60.8 us (97%)
  other arithmetic  1.57 us (3%)
    pallas_call x1, Pallas kernels, per_device(): pl.pallas_call(functools.partial(kernel, n_pool, n_tp), out_shape=jax.Sha...  60.8 us
    reduce_sum x1, other arithmetic, per_device(): return jnp.sum(summands.astype(F32), axis=0)[:, :columns].astype(BF16)  1.57 us

profile of v3, /device:TPU:1, one launch (start us, length us, event | category | flops | bytes accessed | tf_op | source)
XLA Modules:
  0.0 62.3 jit_solution(12033282914516589308)
XLA Ops:
  0.0 60.8 %mla_decode.1 = bf16[32,4,512]{2,1,0:T(4,128)(2,1)} custom-call(s32[64,128]{1,0:T(8,128)} %bitcast.4, s32[128]{0:T(128)} %len_hbm.1, bf16[16,64,576]{2,1,0:T(8,128)(2,1)} %store_hbm.1, bf16[8,2,576]{2,1,0:T(2,128)(2,1)} %query_hbm.1, bf16[2,512,128]{2,1,0:T(8,128)(2,1)} %up_hbm.1, bf16[448,256]{1,0:T(8,128)(2,1)} %bitcast.3), custom_call_target="tpu_custom_call" | custom-call | tf_op jit(solution)/shard_map/mla_decode/pallas_call | solution.py:470
  60.8 1.6 %reduce = bf16[4,512]{1,0:T(4,128)(2,1)} reduce(bf16[32,4,512]{2,1,0:T(4,128)(2,1)} %mla_decode.1, bf16[]{:T(256)} %constant.5), dimensions={0}, to_apply=%region_0.0.clone | reduce | flops 63488 | bytes 135170 | tf_op jit(solution)/shard_map/reduce_sum | solution.py:509

commit v4 on v3

--- a/solution.py
+++ b/solution.py
@@ -211,23 +211,27 @@
             to(tp, to_z * n_y + (y + direction * move + n_y) % n_y),
         )
 
-    def send_pages(role, first, last):
-        def send(i):
-            n = (i + core * (SITE // 2)) % SITE
-            dz, move = route(n)
-            to_z = (z + dz) % 2
-            direction = 1 - 2 * to_z
-            ahead = direction * (1 - 2 * role) * move - direction * (1 - role) * FAR
-            packed(stage.at[role * SITE + n], slot_of(to_z * n_y + (y + ahead + 2 * n_y) % n_y))
-
-            @pl.when(n < SITE - 1)
-            def _():
-                page_copy(role, n).start()
-
-        each(first, last, send)
-        if last == SITE:
-            local = role * SITE + SITE - 1
-            land[local] = stage[local]
+    def page_in_turn(i):
+        return (i + core * (SITE // 2)) % SITE
+
+    def pack_page(role, i):
+        n = page_in_turn(i)
+        dz, move = route(n)
+        to_z = (z + dz) % 2
+        direction = 1 - 2 * to_z
+        ahead = direction * (1 - 2 * role) * move - direction * (1 - role) * FAR
+        packed(stage.at[role * SITE + n], slot_of(to_z * n_y + (y + ahead + 2 * n_y) % n_y))
+
+    def send_page(role, i):
+        n = page_in_turn(i)
+
+        @pl.when(n < SITE - 1)
+        def _():
+            page_copy(role, n).start()
+
+    def pack_and_send(i):
+        pack_page(0, i)
+        send_page(0, i)
 
     loads[2].wait()
     for i in range(requests):
@@ -256,7 +260,11 @@
     start(map(q_copy, X_CORE))
     loads[0].wait()
     loads[1].wait()
-    send_pages(0, 0, SITE // 2)
+    each(0, SITE // 2, pack_and_send)
+    each(SITE // 2, SITE, lambda i: pack_page(0, i))
+    each(0, SITE, lambda i: pack_page(1, i))
+    for role in range(2):
+        land[role * SITE + SITE - 1] = stage[role * SITE + SITE - 1]
 
     q_land[here] = q_msg[pl.ds(x * 2, 2)]
     arrive(map(q_copy, X_CORE))
@@ -289,8 +297,8 @@
     start([query_copy(0, dz) for dz in Z_HI + [0]])
     start([query_copy(1, dz) for dz in Z_HI])
     q_all[1, z_hi] = q_part[z_hi // 2]
-    send_pages(0, SITE // 2, SITE)
-    send_pages(1, 0, SITE)
+    each(SITE // 2, SITE, lambda i: send_page(0, i))
+    each(0, SITE, lambda i: send_page(1, i))
     for load in loads[3:]:
         load.wait()
 

time: 62.5 us -> 62.8 us (level)
  no operation moved by 1% of the time
where the time goes in v4:
time: 62.8 us; the launch traced here: 62.7 us
  Pallas kernels  61.1 us (97%)
  other arithmetic  1.57 us (2%)
    pallas_call x1, Pallas kernels, per_device(): pl.pallas_call(functools.partial(kernel, n_pool, n_tp), out_shape=jax.Sha...  61.1 us
    reduce_sum x1, other arithmetic, per_device(): return jnp.sum(summands.astype(F32), axis=0)[:, :columns].astype(BF16)  1.57 us

profile of v4, /device:TPU:1, one launch (start us, length us, event | category | flops | bytes accessed | tf_op | source)
XLA Modules:
  0.0 62.7 jit_solution(9597642362220641056)
XLA Ops:
  0.0 61.1 %mla_decode.1 = bf16[32,4,512]{2,1,0:T(4,128)(2,1)} custom-call(s32[64,128]{1,0:T(8,128)} %bitcast.4, s32[128]{0:T(128)} %len_hbm.1, bf16[16,64,576]{2,1,0:T(8,128)(2,1)} %store_hbm.1, bf16[8,2,576]{2,1,0:T(2,128)(2,1)} %query_hbm.1, bf16[2,512,128]{2,1,0:T(8,128)(2,1)} %up_hbm.1, bf16[448,256]{1,0:T(8,128)(2,1)} %bitcast.3), custom_call_target="tpu_custom_call" | custom-call | tf_op jit(solution)/shard_map/mla_decode/pallas_call | solution.py:478
  61.1 1.6 %reduce = bf16[4,512]{1,0:T(4,128)(2,1)} reduce(bf16[32,4,512]{2,1,0:T(4,128)(2,1)} %mla_decode.1, bf16[]{:T(256)} %constant.5), dimensions={0}, to_apply=%region_0.0.clone | reduce | flops 63488 | bytes 135170 | tf_op jit(solution)/shard_map/reduce_sum | solution.py:517

commit v5 on v4

--- a/solution.py
+++ b/solution.py
@@ -52,6 +52,7 @@
     up_hbm,
     proj_hbm,
     out_ref,
+    near_hbm,
     table_ref,
     len_ref,
     store_ref,
@@ -59,6 +60,7 @@
     up_ref,
     proj_ref,
     local_sem,
+    near_sem,
     stage,
     land,
     q_msg,
@@ -203,8 +205,9 @@
         dz, move = route(n)
         to_z = (z + dz) % 2
         direction = (1 - 2 * to_z) * (1 - 2 * role)
-        return remote(
-            stage.at[role * SITE + n],
+        source = near_hbm.at[n] if isinstance(role, int) and role == 1 else stage.at[n]
+        return remote(
+            source,
             land.at[role * SITE + n],
             (page_send, page_recv),
             role * SITE + n,
@@ -262,7 +265,16 @@
     loads[1].wait()
     each(0, SITE // 2, pack_and_send)
     each(SITE // 2, SITE, lambda i: pack_page(0, i))
-    each(0, SITE, lambda i: pack_page(1, i))
+
+    def near_copy(i):
+        n = page_in_turn(i)
+        return pltpu.make_async_copy(stage.at[SITE + n], near_hbm.at[n], near_sem.at[i])
+
+    def pack_near(i):
+        pack_page(1, i)
+        near_copy(i).start()
+
+    each(0, SITE, pack_near)
     for role in range(2):
         land[role * SITE + SITE - 1] = stage[role * SITE + SITE - 1]
 
@@ -298,7 +310,12 @@
     start([query_copy(1, dz) for dz in Z_HI])
     q_all[1, z_hi] = q_part[z_hi // 2]
     each(SITE // 2, SITE, lambda i: send_page(0, i))
-    each(0, SITE, lambda i: send_page(1, i))
+
+    def send_near(i):
+        near_copy(i).wait()
+        send_page(1, i)
+
+    each(0, SITE, send_near)
     for load in loads[3:]:
         load.wait()
 
@@ -475,11 +492,15 @@
     hbm = pl.BlockSpec(memory_space=pltpu.HBM)
     message = lambda *lead: pltpu.VMEM((*lead, MSG, LANES), BF16)
     sems = lambda n: [pltpu.SemaphoreType.DMA((n,)), pltpu.SemaphoreType.DMA((n,))]
-    summands = pl.pallas_call(
+    packed_page = (tokens * key_width // LANES, LANES)
+    summands, _ = pl.pallas_call(
         functools.partial(kernel, n_pool, n_tp),
-        out_shape=jax.ShapeDtypeStruct((n_tp, 4, 4 * LANES), BF16),
+        out_shape=[
+            jax.ShapeDtypeStruct((n_tp, 4, 4 * LANES), BF16),
+            jax.ShapeDtypeStruct((SITE, *packed_page), BF16),
+        ],
         in_specs=[hbm] * 6,
-        out_specs=hbm,
+        out_specs=[hbm, hbm],
         scratch_shapes=[
             pltpu.SMEM((n_pool, page_table.shape[0]), jnp.int32),
             pltpu.SMEM(context_len.shape, jnp.int32),
@@ -488,6 +509,7 @@
             pltpu.VMEM(value_up.shape, BF16),
             pltpu.VMEM(out_proj.shape[::-1], BF16),
             pltpu.SemaphoreType.DMA((6,)),
+            pltpu.SemaphoreType.DMA((SITE,)),
             pltpu.VMEM((n_pool, tokens * key_width // LANES, LANES), BF16),
             pltpu.VMEM((n_pool, tokens * key_width // LANES, LANES), BF16),
             message(GROUPS),

time: 62.8 us -> 62.9 us (level)
  no operation moved by 1% of the time
where the time goes in v5:
time: 62.9 us; the launch traced here: 62.8 us
  Pallas kernels  61.2 us (97%)
  other arithmetic  1.57 us (2%)
    pallas_call x1, Pallas kernels, per_device(): pl.pallas_call(functools.partial(kernel, n_pool, n_tp), out_shape=[jax.Sh...  61.2 us
    reduce_sum x1, other arithmetic, per_device(): return jnp.sum(summands.astype(F32), axis=0)[:, :columns].astype(BF16)  1.57 us

profile of v5, /device:TPU:1, one launch (start us, length us, event | category | flops | bytes accessed | tf_op | source)
XLA Modules:
  0.0 62.8 jit_solution(2200054873170235165)
XLA Ops:
  0.0 61.2 %mla_decode.1 = (bf16[32,4,512]{2,1,0:T(4,128)(2,1)}, bf16[8,288,128]{2,1,0:T(8,128)(2,1)}) custom-call(s32[64,128]{1,0:T(8,128)} %bitcast.4, s32[128]{0:T(128)} %len_hbm.1, bf16[16,64,576]{2,1,0:T(8,128)(2,1)} %store_hbm.1, bf16[8,2,576]{2,1,0:T(2,128)(2,1)} %query_hbm.1, bf16[2,512,128]{2,1,0:T(8,128)(2,1)} %up_hbm.1, bf16[448,256]{1,0:T(8,128)(2,1)} %bitcast.3), custom_call_target="tpu_custom_call" | custom-call | tf_op jit(solution)/shard_map/mla_decode/pallas_call | solution.py:496
  61.2 1.6 %reduce = bf16[4,512]{1,0:T(4,128)(2,1)} reduce(bf16[32,4,512]{2,1,0:T(4,128)(2,1)} %get-tuple-element.6, bf16[]{:T(256)} %constant.5), dimensions={0}, to_apply=%region_0.0.clone | reduce | flops 63488 | bytes 135170 | tf_op jit(solution)/shard_map/reduce_sum | solution.py:539

commit v6 on v3

--- a/solution.py
+++ b/solution.py
@@ -256,7 +256,7 @@
     start(map(q_copy, X_CORE))
     loads[0].wait()
     loads[1].wait()
-    send_pages(0, 0, SITE // 2)
+    send_pages(0, 0, 5)
 
     q_land[here] = q_msg[pl.ds(x * 2, 2)]
     arrive(map(q_copy, X_CORE))
@@ -289,7 +289,7 @@
     start([query_copy(0, dz) for dz in Z_HI + [0]])
     start([query_copy(1, dz) for dz in Z_HI])
     q_all[1, z_hi] = q_part[z_hi // 2]
-    send_pages(0, SITE // 2, SITE)
+    send_pages(0, 5, SITE)
     send_pages(1, 0, SITE)
     for load in loads[3:]:
         load.wait()

time: 62.5 us -> 63.2 us (1.011)
  Pallas kernels: 60.8 us -> 61.5 us
    pallas_call x1, Pallas kernels: 60.8 us -> 61.5 us  [per_device(): pl.pallas_call(functools.partial(kernel, n_pool, n_tp), out_shape=jax.Sha...]
where the time goes in v6:
time: 63.2 us; the launch traced here: 63 us
  Pallas kernels  61.5 us (97%)
  other arithmetic  1.57 us (2%)
    pallas_call x1, Pallas kernels, per_device(): pl.pallas_call(functools.partial(kernel, n_pool, n_tp), out_shape=jax.Sha...  61.5 us
    reduce_sum x1, other arithmetic, per_device(): return jnp.sum(summands.astype(F32), axis=0)[:, :columns].astype(BF16)  1.57 us

profile of v6, /device:TPU:1, one launch (start us, length us, event | category | flops | bytes accessed | tf_op | source)
XLA Modules:
  0.0 63.0 jit_solution(8381144772055430137)
XLA Ops:
  0.0 61.5 %mla_decode.1 = bf16[32,4,512]{2,1,0:T(4,128)(2,1)} custom-call(s32[64,128]{1,0:T(8,128)} %bitcast.4, s32[128]{0:T(128)} %len_hbm.1, bf16[16,64,576]{2,1,0:T(8,128)(2,1)} %store_hbm.1, bf16[8,2,576]{2,1,0:T(2,128)(2,1)} %query_hbm.1, bf16[2,512,128]{2,1,0:T(8,128)(2,1)} %up_hbm.1, bf16[448,256]{1,0:T(8,128)(2,1)} %bitcast.3), custom_call_target="tpu_custom_call" | custom-call | tf_op jit(solution)/shard_map/mla_decode/pallas_call | solution.py:470
  61.5 1.6 %reduce = bf16[4,512]{1,0:T(4,128)(2,1)} reduce(bf16[32,4,512]{2,1,0:T(4,128)(2,1)} %mla_decode.1, bf16[]{:T(256)} %constant.5), dimensions={0}, to_apply=%region_0.0.clone | reduce | flops 63488 | bytes 135170 | tf_op jit(solution)/shard_map/reduce_sum | solution.py:509
